TPU v7x, 32 devices: a whole 2x2x4 slice. The times are simulated.
32 devices in a mesh: leaf: 4 (over x, core), row: 2 (over y), col: 4 (over z).
Axes of the slice: x: 2, y: 2, z: 4, core: 2. Of those that a mesh axis runs over, the one named last changes fastest.
Arguments:
- child_front: float32 [4, 4096, 4096], P('leaf', 'row', 'col'), as said below
- parent_front: bfloat16 [8192, 16384], P('row', ('leaf', 'col')), as said below
- block_map: int32 [4, 28], replicated, may hold values from 0 to 63, as said below
Outputs:
- child_panel_t: float32 [4, 512, 4096], P('leaf', 'col', 'row')
- parent_panel_t: float32 [1024, 8192], P(('leaf', 'col'), 'row')
- parent_update: float32 [8192, 16384], P('row', ('leaf', 'col'))
Inputs may be any that keep to these rules, and one draw needn't show every extreme that they name: `child_front`: every child front is symmetric positive definite. `parent_front`: every parent front (each block of 8192 columns) is symmetric positive definite. `block_map`: in each row the entries are distinct. Of the contribution blocks that one device of a child's grid holds in its rows, at most 8 go to parent blocks whose rows one index of row holds; of those it holds in its columns, at most 2 go to parent blocks whose columns are held by one index of col, counting both leaves of the pair together; of all contribution blocks of one child, at most 14 go to parent blocks whose rows one index of row holds. All three bounds are reached.
All inputs are finite; a program needn't handle non-finite values.
Results may differ from a plain program's by a relative error of at most 0.0003.
Values sent between devices are 32-bit elements; how exact they have to be, the bound alone decides.
A program may use at most 192 MiB of HBM per device.

v0:
```python
import jax
import jax.numpy as jnp
from jax import lax
from jax.sharding import PartitionSpec as P

BLK = 128


def from_partner(value, axis, bit):
    mask = 2**bit
    pairs = [(source, source ^ mask) for source in range(lax.axis_size(axis))]
    return lax.ppermute(value, axis, pairs)


def from_root(value, axis, source):
    kept = jnp.where(lax.axis_index(axis) == source, value, 0).astype(value.dtype)
    return lax.psum(kept, axis)


def pair_swap(values):
    return from_partner(values, "leaf", 0)


def one_hot(values, size):
    return (values[:, None] == jnp.arange(size)[None, :]).astype(jnp.float32)


def factor_panel(front_block, panel_width, row_start, col_start, paired):
    precise_setting = lax.Precision.HIGHEST
    panel_slab = from_root(front_block[:, :panel_width], "col", 0)
    if paired:
        partner = pair_swap(panel_slab)
        panel_slab = jnp.where(lax.axis_index("leaf") % 2 == 0, panel_slab, partner)
    block_cols = front_block.shape[1]
    joined = jnp.concatenate((front_block[:panel_width], panel_slab[:panel_width]), axis=1)
    joined = from_root(joined, "row", 0)
    top_block = joined[:, :block_cols]
    diagonal_block = joined[:, block_cols:]
    lower_factor = jnp.linalg.cholesky(diagonal_block)
    identity = jnp.eye(panel_width, dtype=jnp.float32)
    inverse_factor = jax.scipy.linalg.solve_triangular(lower_factor, identity, lower=True)
    rows_factor = jnp.dot(panel_slab, inverse_factor.T, precision=precise_setting)
    cols_factor = jnp.dot(inverse_factor, top_block, precision=precise_setting)
    update = jnp.dot(rows_factor, cols_factor, precision=precise_setting)
    row_ids = row_start + jnp.arange(front_block.shape[0])
    col_ids = col_start + jnp.arange(block_cols)
    keep_mask = (row_ids[:, None] >= panel_width) & (col_ids[None, :] >= panel_width)
    schur_part = jnp.where(keep_mask, front_block - update, jnp.float32(0.0))
    return (rows_factor, schur_part)


def shards(child_front, parent_front, block_map):
    leaf_id = lax.axis_index("leaf")
    row_id = lax.axis_index("row")
    col_id = lax.axis_index("col")
    row_count = lax.axis_size("row")
    col_count = lax.axis_size("col")
    precise_setting = lax.Precision.HIGHEST
    child_block = child_front[0]
    child_rows, child_cols = child_block.shape
    panel_width = child_cols // 2
    rows_factor, contribution = factor_panel(
        child_block, panel_width, row_id * child_rows, col_id * child_cols, False
    )
    out_width = panel_width // col_count
    child_out = lax.dynamic_slice_in_dim(rows_factor, col_id * out_width, out_width, 1).T[None]
    parent_rows, parent_cols = parent_front.shape
    parent_order = parent_rows * row_count
    row_span = parent_rows // BLK
    col_span = parent_cols // BLK
    row_blocks = child_rows // BLK
    col_blocks = child_cols // BLK
    cap_rows = max(1, row_blocks // row_count)
    cap_cols = max(1, col_blocks // col_count)
    own_map = lax.dynamic_index_in_dim(block_map, leaf_id, 0, keepdims=False)
    block_count = own_map.shape[0]
    block_ids = jnp.arange(block_count)
    global_ids = panel_width + block_ids * BLK
    src_row = global_ids // child_rows
    src_col = global_ids // child_cols
    dst_row = own_map // row_span
    owner_col = own_map // col_span
    dst_col = owner_col % col_count
    dst_half = owner_col // col_count
    earlier = block_ids[None, :] < block_ids[:, None]
    rank_row = jnp.sum(
        earlier & (src_row[None, :] == src_row[:, None]) & (dst_row[None, :] == dst_row[:, None]),
        axis=1,
    )
    rank_col = jnp.sum(
        earlier & (src_col[None, :] == src_col[:, None]) & (dst_col[None, :] == dst_col[:, None]),
        axis=1,
    )
    local_rows = (global_ids - row_id * child_rows) // BLK
    local_cols = (global_ids - col_id * child_cols) // BLK
    row_pick = jnp.einsum(
        "k,kd,ka,kx->dax",
        (src_row == row_id).astype(jnp.float32),
        one_hot(dst_row, row_count),
        one_hot(rank_row, cap_rows),
        one_hot(local_rows, row_blocks),
        precision=precise_setting,
    )
    col_pick = jnp.einsum(
        "k,ke,kj,ky->ejy",
        (src_col == col_id).astype(jnp.float32),
        one_hot(dst_col, col_count),
        one_hot(rank_col, cap_cols),
        one_hot(local_cols, col_blocks),
        precision=precise_setting,
    )
    place_cols = jnp.einsum(
        "k,kh,ky,kc,kj->hycj",
        (dst_col == col_id).astype(jnp.float32),
        one_hot(dst_half, 2),
        one_hot(own_map % col_span, col_span),
        one_hot(src_col, col_count),
        one_hot(rank_col, cap_cols),
        precision=precise_setting,
    )
    strip_view = contribution.reshape(row_blocks, BLK, child_cols)
    strips = jnp.einsum("dax,xiw->daiw", row_pick, strip_view, precision=precise_setting)
    received_blocks = lax.all_to_all(
        strips.reshape(row_count, cap_rows * BLK, child_cols),
        "row",
        split_axis=0,
        concat_axis=0,
        tiled=True,
    )
    received_blocks = received_blocks.reshape(row_count, cap_rows, BLK, child_cols)
    on_this_row = (dst_row == row_id).astype(jnp.float32)
    rank_dest = jnp.sum(earlier & (dst_row[None, :] == dst_row[:, None]), axis=1)
    cap_incoming = -(-block_count // row_count)
    dense_selection = jnp.einsum(
        "c,cn,cw,cp->nwp",
        on_this_row,
        one_hot(rank_dest, cap_incoming),
        one_hot(src_row, row_count),
        one_hot(rank_row, cap_rows),
        precision=precise_setting,
    )
    squeezed_result = jnp.einsum(
        "byx,yxhq->bhq", dense_selection, received_blocks, precision=precise_setting
    )
    squeezed_result = squeezed_result.reshape(cap_incoming, BLK, col_blocks, BLK)
    sending = jnp.einsum("miyb,ejy->emijb", squeezed_result, col_pick, precision=precise_setting)
    landed = lax.all_to_all(
        sending.reshape(col_count, cap_incoming * BLK, cap_cols * BLK),
        "col",
        split_axis=0,
        concat_axis=0,
        tiled=True,
    )
    landed = landed.reshape(col_count, cap_incoming, BLK, cap_cols, BLK)
    place_rows = jnp.einsum(
        "k,kx,km->xm",
        on_this_row,
        one_hot(own_map % row_span, row_span),
        one_hot(rank_dest, cap_incoming),
        precision=precise_setting,
    )
    placed_rows = jnp.einsum("xm,cmijb->xcijb", place_rows, landed, precision=precise_setting)
    halves = jnp.einsum(
        "xcijb,hycj->hxiyb", placed_rows, place_cols, precision=precise_setting
    ).reshape(2, parent_rows, parent_cols)
    own_half = leaf_id % 2
    own_part = lax.dynamic_index_in_dim(halves, own_half, 0, keepdims=False)
    other_part = lax.dynamic_index_in_dim(halves, 1 - own_half, 0, keepdims=False)
    assembled = parent_front.astype(jnp.float32) + own_part + pair_swap(other_part)
    parent_width = parent_cols // 2
    col_start = own_half * (parent_order // 2) + col_id * parent_cols
    parent_factor, parent_schur = factor_panel(
        assembled, parent_width, row_id * parent_rows, col_start, True
    )
    share_width = parent_width // (2 * col_count)
    share_start = (own_half * col_count + col_id) * share_width
    parent_out = lax.dynamic_slice_in_dim(parent_factor, share_start, share_width, 1).T
    return (child_out, parent_out, parent_schur)


def solution(mesh):
    placed = (P("leaf", "row", "col"), P("row", ("leaf", "col")), P())
    return jax.shard_map(
        shards,
        mesh=mesh,
        in_specs=placed,
        out_specs=(P("leaf", "col", "row"), P(("leaf", "col"), "row"), P("row", ("leaf", "col"))),
        check_vma=False,
    )
```

profile of v0, /device:TPU:1, one launch (start us, length us, event | category | flops | bytes accessed | tf_op | source)
XLA Modules:
  0.0 1631.4 jit_solution(17223995047964636296)
XLA Ops:
  7.2 9.1 copy.48
  16.3 4.7 slice_select_fusion.1
  21.1 1.8 slice_bitcast_fusion
  22.9 155.4 %all-reduce.6.cloned.1.call-done = f32[2048,512]{0,1:T(8,128)} async-done(((f32[2048,512]{0,1:T(8,128)}), f32[2048,512]{0,1:T(8,128)}) %all-reduce.6.cloned.1.call-update) | async-done | bytes 4194320 | tf_op jit(solution)/shard_map/psum | solution.py:17
  179.6 2.1 maximum_select_fusion
  183.0 83.7 %all-reduce.8.cloned.1.call-done = f32[512,1536]{0,1:T(8,128)} async-done(((f32[512,1536]{0,1:T(8,128)}), f32[512,1536]{0,1:T(8,128)}) %all-reduce.8.cloned.1.call-update) | async-done | bytes 3145744 | tf_op jit(solution)/shard_map/psum | solution.py:17
  268.3 1.4 fusion.18
  269.7 11.7 cholesky.286
  281.6 9.8 custom-call.27
  292.1 11.7 cholesky.305
  303.9 10.0 custom-call.28
  314.5 11.7 cholesky.326
  326.3 9.8 custom-call.29
  336.7 22.5 %cholesky.343 = f32[128,128]{1,0:T(8,128)S(1)} custom-call(f32[128,128]{1,0:T(8,128)S(1)} %convolution_subtract_fusion.11), custom_call_target="Cholesky" | custom-call | tf_op jit(solution)/shard_map/jit(cholesky)/cholesky | solution.py:39
  364.1 8.2 while.4
  372.9 39.3 %custom-call.30 = f32[4,128,128]{1,2,0:T(8,128)S(1)} custom-call(f32[4,128,128]{2,1,0:T(8,128)S(1)} %get-tuple-element.19), custom_call_target="InvertDiagBlocksLowerTriangular" | custom-call | tf_op jit(solution)/shard_map/jit(_solve_triangular)/triangular_solve | solution.py:41
  415.4 13.6 fusion.31
  429.0 3.6 fusion.15
  432.6 15.5 select_bitcast_fusion
  448.2 5.6 copy.79
  453.8 8.8 copy.53
  462.6 11.5 fusion.3
  474.0 8.3 copy.54
  482.3 6.9 all-to-all-start
  489.8 91.2 %all-to-all-done = f32[2,1024,1024]{2,1,0:T(8,128)} async-done(((f32[2,1024,1024]{2,1,0:T(8,128)}), f32[2,1024,1024]{2,1,0:T(8,128)}, u32[]{:S(2)}, u32[]{:S(2)}) %all-to-all-start) | async-done | bytes 8388640 | tf_op jit(solution)/shard_map/all_to_all | solution.py:123
  581.0 9.5 copy.55
  590.5 9.2 copy.56
  599.7 9.5 convolution_bitcast_fusion.1
  609.2 14.0 fusion.10
  623.2 11.7 copy.58
  634.9 10.4 reshape.312
  645.3 5.4 all-to-all-start.1
  651.2 159.6 %all-to-all-done.1 = f32[4,1792,256]{2,1,0:T(8,128)} async-done(((f32[4,1792,256]{2,1,0:T(8,128)}), f32[4,1792,256]{2,1,0:T(8,128)}, u32[]{:S(2)}, u32[]{:S(2)}) %all-to-all-start.1) | async-done | bytes 7340064 | tf_op jit(solution)/shard_map/all_to_all | solution.py:147
  810.9 10.4 reshape.313
  821.3 15.7 fusion.5
  837.0 49.1 %convolution_bitcast_fusion = f32[2,32,128,8,128]{4,3,2,1,0:T(8,128)} fusion(f32[2,8,4,2,1,1]{1,2,3,5,4,0:T(4,128)S(1)} %convolution_bitcast_fusion.2, f32[32,4,128,2,128]{4,0,3,2,1:T(8,128)S(1)} %fusion.5), kind=kOutput, calls=%fused_computation.4 | convolution fusion | flops 805306368 | bytes 50332160 | tf_op jit(solution)/shard_map/xcijb,hycj->hxiyb/dot_general | solution.py:163
  886.0 35.5 %reshape.314 = f32[2,4096,1024]{2,1,0:T(8,128)} reshape(f32[2,32,128,8,128]{4,3,2,1,0:T(8,128)} %convolution_bitcast_fusion) | data formatting | bytes 67108864 | tf_op jit(solution)/shard_map/reshape | solution.py:165
  921.5 21.8 %constant_dynamic-slice_fusion.3 = (f32[1,4096,1024]{2,1,0:T(8,128)}, f32[1,4096,1024]{2,1,0:T(8,128)}) fusion(f32[2,4096,1024]{2,1,0:T(8,128)} %reshape.314, s32[]{:T(128)S(6)} %select_n.201, s32[]{:T(128)S(6)} %select_n.202), kind=kLoop, calls=%fused_computation.228 | loop fusion | bytes 67108872 | tf_op jit(solution)/shard_map/jit(dynamic_index_in_dim)/dynamic_slice | solution.py:167
  943.3 17.5 %copy.78 = f32[1,4096,1024]{1,2,0:T(8,128)} copy(f32[1,4096,1024]{2,1,0:T(8,128)} %get-tuple-element.64) | data formatting | bytes 33554432
  960.8 1.5 collective-permute-start
  962.3 11.5 copy.51
  973.8 17.5 %copy.77 = f32[1,4096,1024]{1,2,0:T(8,128)} copy(f32[1,4096,1024]{2,1,0:T(8,128)} %get-tuple-element.63) | data formatting | bytes 33554432
  991.2 14.2 fusion
  1005.4 6.2 copy-done
  1011.6 3.8 slice_select_fusion
  1015.9 288.2 %all-reduce.10.cloned.1.call-done = f32[4096,512]{0,1:T(8,128)} async-done(((f32[4096,512]{0,1:T(8,128)}), f32[4096,512]{0,1:T(8,128)}) %all-reduce.10.cloned.1.call-update) | async-done | bytes 8388624 | tf_op jit(solution)/shard_map/psum | solution.py:17
  1304.8 13.1 collective-permute-done.1
  1317.9 8.8 broadcast_select_fusion
  1328.0 2.1 maximum_select_fusion.1
  1332.8 82.0 %all-reduce.12.cloned.1.call-done = f32[512,1536]{0,1:T(8,128)} async-done(((f32[512,1536]{0,1:T(8,128)}), f32[512,1536]{0,1:T(8,128)}) %all-reduce.12.cloned.1.call-update) | async-done | bytes 3145744 | tf_op jit(solution)/shard_map/psum | solution.py:17
  1416.4 1.4 fusion.17
  1417.9 11.7 cholesky.358
  1429.7 9.8 custom-call.31
  1440.2 11.9 cholesky.377
  1452.1 9.8 custom-call.32
  1462.6 11.7 cholesky.398
  1474.4 9.8 custom-call.33
  1484.8 12.1 cholesky.415
  1502.4 8.2 while.5
  1510.6 39.3 %custom-call.34 = f32[4,128,128]{1,2,0:T(8,128)S(1)} custom-call(f32[4,128,128]{2,1,0:T(8,128)S(1)} %get-tuple-element.20), custom_call_target="InvertDiagBlocksLowerTriangular" | custom-call | tf_op jit(solution)/shard_map/jit(_solve_triangular)/triangular_solve | solution.py:41
  1553.1 17.7 %fusion.30 = f32[4096,512]{0,1:T(8,128)S(1)} fusion(f32[4096,512]{0,1:T(8,128)} %broadcast_select_fusion, f32[128,512]{1,0:T(8,128)S(1)} %fusion.58, f32[128,512]{1,0:T(8,128)S(1)} %fusion.59, f32[128,512]{1,0:T(8,128)S(1)} %fusion.61, f32[128,512]{1,0:T(8,128)S(1)} %fusion.40), kind=kOutput, calls=%fused_computation.74 | convolution fusion | flops 12885688320 | bytes 17825792 | tf_op jit(solution)/shard_map/dot_general | solution.py:42
  1571.9 3.6 fusion.13
  1575.5 31.7 %subtract_select_fusion = f32[4096,1024]{0,1:T(8,128)} fusion(f32[4096,1024]{0,1:T(8,128)S(1)} %bitcast.237, pred[4096]{0:T(1024)(128)(4,1)S(1)} %add_compare_fusion, pred[1024]{0:T(1024)(128)(4,1)S(1)} %add_compare_fusion.2, f32[4096,512]{0,1:T(8,128)S(1)} %fusion.30, f32[512,1024]{1,0:T(8,128)S(1)} %fusion.13), kind=kOutput, calls=%fused_computation.9 | convolution fusion | flops 25782386688 | bytes 44045312 | tf_op jit(solution)/shard_map/dot_general | solution.py:44
  1607.3 17.4 %copy.66 = f32[4096,1024]{1,0:T(8,128)} copy(f32[4096,1024]{0,1:T(8,128)} %subtract_select_fusion) | data formatting | bytes 33554432
  (160 shorter events, 45.4 us)
Async XLA Ops:
  7.2 171.1 %all-reduce.6.cloned.1.call-start = ((), (), s32[]{:S(2)}) async-start(), calls=%async_computation.2 | async-start | bytes 8388608 | tf_op jit(solution)/shard_map/psum | solution.py:17
  21.1 245.6 %all-reduce.8.cloned.1.call-start = ((), (), s32[]{:S(2)}) async-start(), calls=%async_computation.3 | async-start | bytes 6291456 | tf_op jit(solution)/shard_map/psum | solution.py:17
  183.0 231.3 %copy-start.3 = (f32[512,512]{1,0:T(8,128)}, f32[512,512]{1,0:T(8,128)S(1)}, u32[]{:S(2)}) copy-start(f32[512,512]{1,0:T(8,128)S(1)} %fusion.19) | copy-start | bytes 3145732
  372.3 0.6 copy-start.7
  412.2 3.2 copy-start.2
  413.8 15.2 copy-start.5
  414.9 17.7 %slice-start.5 = ((s8[8388608]{0:T(1024)(128)(4,1)}), s8[4194304]{0:T(1024)(128)(4,1)S(1)}, s32[]{:S(2)}) async-start(s8[8388608]{0:T(1024)(128)(4,1)} %bitcast.239), calls=%async_computation.11 | async-start | bytes 8388608
  415.4 17.3 %slice-start.6 = ((s8[8388608]{0:T(1024)(128)(4,1)}), s8[4194304]{0:T(1024)(128)(4,1)S(1)}, s32[]{:S(2)}) async-start(s8[8388608]{0:T(1024)(128)(4,1)} %bitcast.239), calls=%async_computation.12 | async-start | bytes 8388608
  429.0 3.6 copy-start.1
  482.3 98.7 %all-to-all-start = ((f32[2,1024,1024]{2,1,0:T(8,128)}), f32[2,1024,1024]{2,1,0:T(8,128)}, u32[]{:S(2)}, u32[]{:S(2)}) async-start(f32[2,1024,1024]{2,1,0:T(8,128)} %bitcast.241), calls=%async_computation | async-start | bytes 16777216 | tf_op jit(solution)/shard_map/all_to_all | solution.py:123
  645.3 165.6 %all-to-all-start.1 = ((f32[4,1792,256]{2,1,0:T(8,128)}), f32[4,1792,256]{2,1,0:T(8,128)}, u32[]{:S(2)}, u32[]{:S(2)}) async-start(f32[4,1792,256]{2,1,0:T(8,128)} %reshape.312), calls=%async_computation.1 | async-start | bytes 14680064 | tf_op jit(solution)/shard_map/all_to_all | solution.py:147
  650.8 653.3 %all-reduce.10.cloned.1.call-start = ((), (), s32[]{:S(2)}) async-start(), calls=%async_computation.4 | async-start | bytes 16777216 | tf_op jit(solution)/shard_map/psum | solution.py:17
  960.8 30.4 %collective-permute-start = (f32[4096,1024]{0,1:T(8,128)}, f32[4096,1024]{0,1:T(8,128)}, u32[]{:S(2)}, u32[]{:S(2)}) collective-permute-start(f32[4096,1024]{0,1:T(8,128)} %bitcast.244), channel_id=1, source_target_pairs={{0,8},{8,0},{16,24},{24,16},{1,9},{9,1},{17,25},{25,17},{2,10},{10... | collective-permute-start | bytes 50331656 | tf_op jit(solution)/shard_map/ppermute | solution.py:12
  1005.4 6.2 copy-start
  1015.4 399.3 %all-reduce.12.cloned.1.call-start = ((), (), s32[]{:S(2)}) async-start(), calls=%async_computation.5 | async-start | bytes 6291456 | tf_op jit(solution)/shard_map/psum | solution.py:17
  1304.1 13.8 collective-permute-start.1
  1304.8 23.2 %slice-start.4 = ((f32[4096,1024]{0,1:T(8,128)}), f32[512,1024]{0,1:T(8,128)S(1)}, s32[]{:S(2)}) async-start(f32[4096,1024]{0,1:T(8,128)} %copy-done), calls=%async_computation.10 | async-start | bytes 4194304 | tf_op jit(solution)/shard_map/slice | solution.py:35
  1331.5 170.9 %copy-start.8 = (s32[4,2]{0,1:T(2,128)S(1)}, s32[4,2]{0,1:T(2,128)}, u32[]{:S(2)}) copy-start(s32[4,2]{0,1:T(2,128)} %copy-done.7) | copy-start | bytes 100
  1331.5 218.4 %copy-start.4 = (f32[512,512]{1,0:T(8,128)S(1)}, f32[512,512]{1,0:T(8,128)}, u32[]{:S(2)}) copy-start(f32[512,512]{1,0:T(8,128)} %copy-done.3) | copy-start | bytes 3145732
  1550.4 25.1 %slice-start = ((s8[16777216]{0:T(1024)(128)(4,1)}), s8[4194304]{0:T(1024)(128)(4,1)S(1)}, s32[]{:S(2)}) async-start(s8[16777216]{0:T(1024)(128)(4,1)} %bitcast.236), calls=%async_computation.6 | async-start | bytes 8388608
  1553.1 18.8 %copy-start.6 = (f32[512,1536]{0,1:T(8,128)S(1)}, f32[512,1536]{0,1:T(8,128)}, u32[]{:S(2)}) copy-start(f32[512,1536]{0,1:T(8,128)} %all-reduce.12.cloned.1.call-done) | copy-start | bytes 9437188
  1553.1 22.4 %slice-start.1 = ((s8[16777216]{0:T(1024)(128)(4,1)}), s8[4194304]{0:T(1024)(128)(4,1)S(1)}, s32[]{:S(2)}) async-start(s8[16777216]{0:T(1024)(128)(4,1)} %bitcast.236), calls=%async_computation.7 | async-start | bytes 8388608
  1553.1 22.4 %slice-start.2 = ((s8[16777216]{0:T(1024)(128)(4,1)}), s8[4194304]{0:T(1024)(128)(4,1)S(1)}, s32[]{:S(2)}) async-start(s8[16777216]{0:T(1024)(128)(4,1)} %bitcast.236), calls=%async_computation.8 | async-start | bytes 8388608
  1553.1 22.4 %slice-start.3 = ((s8[16777216]{0:T(1024)(128)(4,1)}), s8[4194304]{0:T(1024)(128)(4,1)S(1)}, s32[]{:S(2)}) async-start(s8[16777216]{0:T(1024)(128)(4,1)} %bitcast.236), calls=%async_computation.9 | async-start | bytes 8388608
Sparse Core Ops, SparseCore 0:
  21.2 157.0 all-reduce.5
  181.8 84.7 all-reduce.7
  1015.6 288.5 all-reduce.9
  1330.2 84.4 all-reduce.11
where the time goes:
time: 1640 us; the launch traced here: 1630 us
  waiting for transfers between devices  873 us (53%)
  other arithmetic  288 us (18%)
  local copies, waits for them, and re-layouts  239 us (15%)
  matrix products  196 us (12%)
  between operations  20 us (1%)
    psum x4, waiting for transfers between devices, from_root(): return lax.psum(kept, axis)  609 us
    another operation x29, other arithmetic, factor_panel(): lower_factor = jnp.linalg.cholesky(diagonal_block)  169 us
    all_to_all x1, waiting for transfers between devices, shards(): lax.all_to_all(sending.reshape(col_count, cap_incoming * BLK, cap_cols *...  160 us
    all_to_all x1, waiting for transfers between devices, shards(): lax.all_to_all(strips.reshape(row_count, cap_rows * BLK, child_cols), 'ro...  91.2 us
    unnamed x37, local copies, waits for them, and re-layouts  86.7 us
    another operation x5, other arithmetic, factor_panel(): jax.scipy.linalg.solve_triangular(lower_factor, identity, lower=True)  78.9 us
    dot_general x1, matrix products, shards(): jnp.einsum('xcijb,hycj->hxiyb', placed_rows, place_cols, precision=precis...  49.1 us
    dot_general x2, matrix products, factor_panel(): update = jnp.dot(rows_factor, cols_factor, precision=precise_setting)  47.3 us
  transfers between devices with their start and end apart: 8, of which 7 were waited for; matrix products, arithmetic and copies ran while one was open for 2% of the time, Pallas kernels for 0%

commit v1 on v0

v1 whole, which is shorter than its diff:
```python
import functools

import jax
import jax.numpy as jnp
from jax import lax
from jax.experimental import pallas as pl
from jax.experimental.pallas import tpu as pltpu
from jax.sharding import PartitionSpec as P

BLK = 128
HIGH = lax.Precision.HIGH
HIGHEST = lax.Precision.HIGHEST
VMEM_BYTES = 40 * 1024 * 1024


def from_root(value, axes, is_root):
    return lax.psum(jnp.where(is_root, value, jnp.zeros_like(value)), axes)


def pair_swap(value):
    pairs = [(source, source ^ 1) for source in range(lax.axis_size("leaf"))]
    return lax.ppermute(value, "leaf", pairs)


def shift_rows(value, step):
    count = lax.axis_size("row")
    return lax.ppermute(value, "row", [(s, (s + step) % count) for s in range(count)])


def params():
    return pltpu.CompilerParams(vmem_limit_bytes=VMEM_BYTES)


def eliminate_block(block):
    groups = [block[8 * g : 8 * g + 8, :] for g in range(BLK // 8)]
    lanes = lax.broadcasted_iota(jnp.int32, (1, BLK), 1)
    subs = lax.broadcasted_iota(jnp.int32, (8, 1), 0)
    for j in range(BLK):
        first, sub = j // 8, j % 8
        pivot_row = groups[first][sub : sub + 1, :]
        pivot = pivot_row[:, j : j + 1]
        scaled = jnp.where(lanes == j, pivot + 1.0, pivot_row) / pivot
        for g in range(first, BLK // 8):
            column = groups[g][:, j : j + 1]
            if g == first:
                if sub == 7:
                    continue
                column = jnp.where(subs > sub, column, 0.0)
            groups[g] = groups[g] - column * scaled
    full = jnp.concatenate(groups, axis=0)
    rows = lax.broadcasted_iota(jnp.int32, (BLK, BLK), 0)
    cols = lax.broadcasted_iota(jnp.int32, (BLK, BLK), 1)
    diagonal = jnp.sum(jnp.where(rows == cols, full, 0.0), axis=1, keepdims=True)
    unit = jnp.where(rows == cols, 1.0, jnp.where(cols < rows, full, 0.0))
    return unit * lax.rsqrt(diagonal)


def inverse_kernel(block_ref, out_ref, work):
    width = block_ref.shape[0]
    count = width // BLK
    work[...] = block_ref[...]
    row_ids = lax.broadcasted_iota(jnp.int32, (width, width), 0)
    col_ids = lax.broadcasted_iota(jnp.int32, (width, width), 1)
    out_ref[...] = jnp.where(row_ids == col_ids, 1.0, 0.0).astype(jnp.float32)
    for k in range(count):
        low, high = k * BLK, (k + 1) * BLK
        small = eliminate_block(work[low:high, low:high])
        out_ref[low:high, :high] = jnp.dot(
            small, out_ref[low:high, :high], precision=HIGHEST, preferred_element_type=jnp.float32
        )
        if high == width:
            continue
        upper = jnp.dot(
            small, work[low:high, high:], precision=HIGHEST, preferred_element_type=jnp.float32
        )
        lower = upper.T
        work[high:, high:] = work[high:, high:] - jnp.dot(
            lower, upper, precision=HIGHEST, preferred_element_type=jnp.float32
        )
        out_ref[high:, :high] = out_ref[high:, :high] - jnp.dot(
            lower, out_ref[low:high, :high], precision=HIGHEST, preferred_element_type=jnp.float32
        )


def inverse_factor_of(diagonal_block):
    width = diagonal_block.shape[0]
    return pl.pallas_call(
        inverse_kernel,
        out_shape=jax.ShapeDtypeStruct((width, width), jnp.float32),
        in_specs=[pl.BlockSpec(memory_space=pltpu.VMEM)],
        out_specs=pl.BlockSpec(memory_space=pltpu.VMEM),
        scratch_shapes=[pltpu.VMEM((width, width), jnp.float32)],
        compiler_params=params(),
        cost_estimate=pl.CostEstimate(
            flops=60_000_000_000, bytes_accessed=width * width * 8, transcendentals=0
        ),
        name="inverse_factor",
    )(diagonal_block)


def split_parts(value):
    head = value.astype(jnp.bfloat16)
    tail = (value - head.astype(jnp.float32)).astype(jnp.bfloat16)
    return head, tail


def three_dots(rows, cols_head, cols_tail):
    head, tail = split_parts(rows)
    dot = functools.partial(jnp.dot, preferred_element_type=jnp.float32)
    return dot(head, cols_head) + (dot(head, cols_tail) + dot(tail, cols_head))


def child_schur_kernel(
    row_pick, col_pick, front_ref, rows_ref, cols_ref, out_ref, cols_head, cols_tail, schur
):
    @pl.when((pl.program_id(0) == 0) & (pl.program_id(1) == 0))
    def _():
        cols_head[...], cols_tail[...] = split_parts(cols_ref[...])

    schur[...] = front_ref[...] - three_dots(rows_ref[...], cols_head[...], cols_tail[...])
    cap_cols = out_ref.shape[1]
    for j in range(cap_cols):
        for e in range(out_ref.shape[4] // BLK):
            start = pl.multiple_of(col_pick[e * cap_cols + j] * BLK, BLK)
            out_ref[0, j, 0, :, e * BLK : (e + 1) * BLK] = schur[:, pl.ds(start, BLK)]


def child_strips(front, rows_factor, cols_factor, row_pick, col_pick):
    row_count, cap_rows = row_pick.shape
    col_count, cap_cols = col_pick.shape
    width, cols = cols_factor.shape
    grid_spec = pltpu.PrefetchScalarGridSpec(
        num_scalar_prefetch=2,
        grid=(row_count, cap_rows),
        in_specs=[
            pl.BlockSpec((BLK, cols), lambda t, a, rp, cp: (rp[t * cap_rows + a], 0)),
            pl.BlockSpec((BLK, width), lambda t, a, rp, cp: (rp[t * cap_rows + a], 0)),
            pl.BlockSpec((width, cols), lambda t, a, rp, cp: (0, 0)),
        ],
        out_specs=pl.BlockSpec(
            (1, cap_cols, 1, BLK, col_count * BLK), lambda t, a, rp, cp: (t, 0, a, 0, 0)
        ),
        scratch_shapes=[
            pltpu.VMEM((width, cols), jnp.bfloat16),
            pltpu.VMEM((width, cols), jnp.bfloat16),
            pltpu.VMEM((BLK, cols), jnp.float32),
        ],
    )
    return pl.pallas_call(
        child_schur_kernel,
        grid_spec=grid_spec,
        out_shape=jax.ShapeDtypeStruct(
            (row_count, cap_cols, cap_rows, BLK, col_count * BLK), jnp.float32
        ),
        compiler_params=params(),
        name="child_schur",
    )(row_pick.reshape(-1), col_pick.reshape(-1), front, rows_factor, cols_factor)


def parent_schur_kernel(starts, front_ref, rows_ref, cols_ref, out_ref, cols_head, cols_tail):
    step = pl.program_id(0)

    @pl.when(step == 0)
    def _():
        cols_head[...], cols_tail[...] = split_parts(cols_ref[...])

    width = cols_ref.shape[0]
    shape = out_ref.shape
    row_ids = starts[0] + step * shape[0] + lax.broadcasted_iota(jnp.int32, (shape[0], 1), 0)
    col_ids = starts[1] + lax.broadcasted_iota(jnp.int32, (1, shape[1]), 1)
    update = three_dots(rows_ref[...], cols_head[...], cols_tail[...])
    keep = (row_ids >= width) & (col_ids >= width)
    out_ref[...] = jnp.where(keep, front_ref[...] - update, 0.0)


def parent_schur_of(front, rows_factor, cols_factor, starts):
    rows, cols = front.shape
    width = cols_factor.shape[0]
    tile = 2 * BLK
    grid_spec = pltpu.PrefetchScalarGridSpec(
        num_scalar_prefetch=1,
        grid=(rows // tile,),
        in_specs=[
            pl.BlockSpec((tile, cols), lambda i, s: (i, 0)),
            pl.BlockSpec((tile, width), lambda i, s: (i, 0)),
            pl.BlockSpec((width, cols), lambda i, s: (0, 0)),
        ],
        out_specs=pl.BlockSpec((tile, cols), lambda i, s: (i, 0)),
        scratch_shapes=[
            pltpu.VMEM((width, cols), jnp.bfloat16),
            pltpu.VMEM((width, cols), jnp.bfloat16),
        ],
    )
    return pl.pallas_call(
        parent_schur_kernel,
        grid_spec=grid_spec,
        out_shape=jax.ShapeDtypeStruct((rows, cols), jnp.float32),
        compiler_params=params(),
        name="parent_schur",
    )(starts, front, rows_factor, cols_factor)


def squeeze_kernel(source, *refs):
    ins, out_ref = refs[:-1], refs[-1]
    step = pl.program_id(0)
    for t, ref in enumerate(ins):

        @pl.when(source[2 * step] == t)
        def _(ref=ref):
            for e in range(out_ref.shape[0]):
                out_ref[e, 0] = ref[0, :, e * BLK : (e + 1) * BLK]


def squeeze_rows(parts, source):
    incoming = source.shape[0]
    cols = parts[0].shape[2]
    count = cols // BLK
    grid_spec = pltpu.PrefetchScalarGridSpec(
        num_scalar_prefetch=1,
        grid=(incoming,),
        in_specs=[pl.BlockSpec((1, BLK, cols), lambda m, s: (s[2 * m + 1], 0, 0)) for _ in parts],
        out_specs=pl.BlockSpec((count, 1, BLK, BLK), lambda m, s: (0, m, 0, 0)),
    )
    return pl.pallas_call(
        squeeze_kernel,
        grid_spec=grid_spec,
        out_shape=jax.ShapeDtypeStruct((count, incoming, BLK, BLK), jnp.float32),
        compiler_params=params(),
        name="squeeze_rows",
    )(source.reshape(-1), *parts)


def extend_add_kernel(cap_cols, row_from, col_from, front_ref, *refs):
    pieces, out_ref = refs[:-1], refs[-1]
    step = pl.program_id(0)
    span = out_ref.shape[1] // BLK
    for y in range(span):
        lanes = slice(y * BLK, (y + 1) * BLK)
        total = front_ref[:, lanes].astype(jnp.float32)
        for child in range(2):
            valid_row = row_from[child * pl.num_programs(0) + step] >= 0
            for j in range(cap_cols):
                place = col_from[(child * cap_cols + j) * span + y]
                tile = pieces[child * cap_cols + j][jnp.maximum(place, 0), 0]
                total = total + jnp.where(valid_row & (place >= 0), tile, 0.0)
        out_ref[:, lanes] = total


def extend_add(front, pieces, row_from, col_from):
    rows, cols = front.shape
    cap_cols = col_from.shape[1]
    blocks = rows // BLK
    count = pieces[0].shape[0]

    def piece_spec(child):
        return pl.BlockSpec(
            (count, 1, BLK, BLK),
            lambda x, rf, cf: (0, jnp.maximum(rf[child * blocks + x], 0), 0, 0),
        )

    grid_spec = pltpu.PrefetchScalarGridSpec(
        num_scalar_prefetch=2,
        grid=(blocks,),
        in_specs=[pl.BlockSpec((BLK, cols), lambda x, rf, cf: (x, 0))]
        + [piece_spec(child) for child in range(2) for _ in range(cap_cols)],
        out_specs=pl.BlockSpec((BLK, cols), lambda x, rf, cf: (x, 0)),
    )
    return pl.pallas_call(
        functools.partial(extend_add_kernel, cap_cols),
        grid_spec=grid_spec,
        out_shape=jax.ShapeDtypeStruct((rows, cols), jnp.float32),
        compiler_params=params(),
        name="extend_add",
    )(row_from.reshape(-1), col_from.reshape(-1), front, *pieces)


def find(match, values, missing):
    found = jnp.sum(jnp.where(match, values, 0), axis=-1)
    return jnp.where(jnp.any(match, axis=-1), found, missing).astype(jnp.int32)


def ranks(group):
    ids = jnp.arange(group.shape[0])
    earlier = ids[None, :] < ids[:, None]
    return jnp.sum(earlier & (group[None, :] == group[:, None]), axis=1)


def shards(child_front, parent_front, block_map):
    leaf_id = lax.axis_index("leaf")
    row_id = lax.axis_index("row")
    col_id = lax.axis_index("col")
    row_count = lax.axis_size("row")
    col_count = lax.axis_size("col")
    own_half = leaf_id % 2

    child_block = child_front[0]
    child_rows, child_cols = child_block.shape
    width = child_cols // 2
    at_corner = (row_id == 0) & (col_id == 0)
    diagonal = from_root(child_block[:width, :width], ("row", "col"), at_corner)
    child_block, diagonal = lax.optimization_barrier((child_block, diagonal))
    slab = from_root(child_block[:, :width], "col", col_id == 0)
    top = from_root(child_block[:width], "row", row_id == 0)
    inverse = inverse_factor_of(diagonal)
    cols_factor = jnp.dot(inverse, top, precision=HIGH)
    rows_factor = jnp.dot(slab, inverse.T, precision=HIGH)
    out_width = width // col_count
    inverse_share = lax.dynamic_slice_in_dim(inverse, col_id * out_width, out_width, 0)
    child_out = lax.dot_general(inverse_share, slab, (((1,), (1,)), ((), ())), precision=HIGH)[None]

    parent_rows, parent_cols = parent_front.shape
    parent_order = parent_rows * row_count
    row_span = parent_rows // BLK
    col_span = parent_cols // BLK
    cap_rows = max(1, child_rows // BLK // row_count)
    cap_cols = max(1, child_cols // BLK // col_count)
    block_count = block_map.shape[1]
    cap_incoming = -(-block_count // row_count)
    global_ids = width + jnp.arange(block_count) * BLK
    src_row = global_ids // child_rows
    src_col = global_ids // child_cols

    def routes(mapping):
        dst_row = mapping // row_span
        owner = mapping // col_span
        rank_row = ranks(src_row * row_count + dst_row)
        rank_col = ranks(src_col * col_count + owner % col_count)
        return dst_row, owner, rank_row, rank_col, ranks(dst_row)

    own_map = lax.dynamic_index_in_dim(block_map, leaf_id, 0, keepdims=False)
    pair_map = lax.dynamic_index_in_dim(block_map, leaf_id ^ 1, 0, keepdims=False)
    dst_row, owner, rank_row, rank_col, rank_dest = routes(own_map)
    distance = jnp.arange(row_count)[:, None, None]
    row_pick = find(
        (src_row == row_id)
        & (dst_row == (row_id + distance) % row_count)
        & (rank_row == jnp.arange(cap_rows)[None, :, None]),
        (global_ids - row_id * child_rows) // BLK,
        0,
    )
    col_pick = find(
        (src_col == col_id)
        & (owner % col_count == jnp.arange(col_count)[:, None, None])
        & (rank_col == jnp.arange(cap_cols)[None, :, None]),
        (global_ids - col_id * child_cols) // BLK,
        0,
    )
    incoming = (dst_row == row_id) & (rank_dest == jnp.arange(cap_incoming)[:, None])
    source = jnp.stack(
        [find(incoming, (row_id - src_row) % row_count, 0), find(incoming, rank_row, 0)], axis=1
    )
    row_from, col_from = [], []
    for mapping in (own_map, pair_map):
        to_row, to_owner, _, to_rank_col, to_rank_dest = routes(mapping)
        row_from.append(
            find(
                (to_row == row_id) & (mapping % row_span == jnp.arange(row_span)[:, None]),
                to_rank_dest,
                -1,
            )
        )
        col_from.append(
            find(
                (to_owner == own_half * col_count + col_id)
                & (mapping % col_span == jnp.arange(col_span)[:, None])
                & (to_rank_col == jnp.arange(cap_cols)[:, None, None]),
                src_col,
                -1,
            )
        )
    row_from = jnp.stack(row_from)
    col_from = jnp.stack(col_from)

    strips = child_strips(child_block, rows_factor, cols_factor, row_pick, col_pick)
    own_pieces, pair_pieces = [], []
    for j in range(cap_cols):
        parts = [strips[0, j]] + [shift_rows(strips[t, j], t) for t in range(1, row_count)]
        sending = squeeze_rows(parts, source)
        landed = lax.all_to_all(
            sending.reshape(col_count, cap_incoming * BLK, BLK),
            "col",
            split_axis=0,
            concat_axis=0,
            tiled=True,
        ).reshape(col_count, cap_incoming, BLK, BLK)
        own_pieces.append(landed)
        pair_pieces.append(pair_swap(landed))
    assembled = extend_add(parent_front, own_pieces + pair_pieces, row_from, col_from)

    parent_width = parent_cols // 2
    corner = from_root(
        assembled[:parent_width, :parent_width], ("row", "col"), at_corner
    )
    corner = jnp.where(own_half == 0, corner, pair_swap(corner))
    strip, corner = lax.optimization_barrier((assembled[:parent_width], corner))
    parent_top = from_root(strip, "row", row_id == 0)
    if row_count == 2:
        part = parent_width // 2
        kept = jnp.where(own_half == 0, parent_top[:part], parent_top[part:])
        given = jnp.where(own_half == 0, parent_top[part:], parent_top[:part])
        kept = jnp.where(own_half == row_id, kept, pair_swap(given))
        gathered = lax.all_gather(kept, "col")
        other = pair_swap(gathered)
        first = jnp.where(own_half == 0, gathered, other)
        second = jnp.where(own_half == 0, other, gathered)
        panel_t = jnp.concatenate((first, second), axis=1)
    else:
        panel = from_root(assembled[:, :parent_width], "col", col_id == 0)
        panel = jnp.where(own_half == 0, panel, pair_swap(panel))
        panel_t = panel.T[None]
    parent_inverse = inverse_factor_of(corner)
    parent_cols_factor = jnp.dot(parent_inverse, parent_top, precision=HIGH)
    parent_rows_factor = jnp.einsum("cks,pk->csp", panel_t, parent_inverse, precision=HIGH)
    parent_rows_factor = parent_rows_factor.reshape(parent_rows, parent_width)
    share_width = parent_width // (2 * col_count)
    share_start = (own_half * col_count + col_id) * share_width
    share = lax.dynamic_slice_in_dim(parent_inverse, share_start, share_width, 0)
    parent_out = jnp.einsum("qk,cks->qcs", share, panel_t, precision=HIGH)
    parent_out = parent_out.reshape(share_width, parent_rows)
    col_start = own_half * (parent_order // 2) + col_id * parent_cols
    starts = jnp.stack([row_id * parent_rows, col_start]).astype(jnp.int32)
    parent_schur = parent_schur_of(assembled, parent_rows_factor, parent_cols_factor, starts)
    return (child_out, parent_out, parent_schur)


def solution(mesh):
    placed = (P("leaf", "row", "col"), P("row", ("leaf", "col")), P())
    return jax.shard_map(
        shards,
        mesh=mesh,
        in_specs=placed,
        out_specs=(P("leaf", "col", "row"), P(("leaf", "col"), "row"), P("row", ("leaf", "col"))),
        check_vma=False,
    )
```

time: 1640 us -> 965 us (0.59)
  other arithmetic: 288 us -> 27.1 us
  local copies, waits for them, and re-layouts: 239 us -> 17 us
  waiting for transfers between devices: 873 us -> 673 us
  Pallas kernels: 0 us -> 170 us
  matrix products: 196 us -> 33.5 us
    another operation x40 -> x4, other arithmetic: 248 us -> 0.1 us  [the longest x1 0.08 us: shards(): starts = jnp.stack([row_id * parent_rows, col_start]).astype(jnp.int32)]
    psum x4 -> x5, waiting for transfers between devices: 609 us -> 388 us  [from_root(): return lax.psum(jnp.where(is_root, value, jnp.zeros_like(value)), axes)]
    pallas_call x0 -> x7, Pallas kernels: none -> 170 us  [the longest x2 91.9 us: inverse_factor_of(): pl.pallas_call(inverse_kernel, out_shape=jax.ShapeDtypeStruct((width, wid...]
    dot_general x15 -> x6, matrix products: 186 us -> 33.5 us  [the longest x1 14.3 us: shards(): jnp.einsum('cks,pk->csp', panel_t, parent_inverse, precision=HIGH)]
    all_to_all x2, waiting for transfers between devices: 251 us -> 112 us  [shards(): lax.all_to_all(sending.reshape(col_count, cap_incoming * BLK, BLK), 'col'...]
    ppermute x2 -> x7, waiting for transfers between devices: 13.1 us -> 97.4 us  [the longest x2 89.3 us: shift_rows(): lax.ppermute(value, 'row', [(s, (s + step) % count) for s in range(count)])]
    unnamed x37 -> x14, local copies, waits for them, and re-layouts: 86.7 us -> 7.02 us
    all_gather x0 -> x1, waiting for transfers between devices: none -> 75.2 us  [shards(): gathered = lax.all_gather(kept, 'col')]
  transfers between devices with their start and end apart: 8 -> 15, of which waited for: 7 -> 13; matrix products, arithmetic and copies ran while one was open for 2% -> 2% of each run, Pallas kernels for 0% -> 10%
where the time goes in v1:
time: 965 us; the launch traced here: 953 us
  waiting for transfers between devices  673 us (70%)
  Pallas kernels  170 us (18%)
  matrix products  33.5 us (3%)
  other arithmetic  27.1 us (3%)
  starting transfers between devices  18.5 us (2%)
  local copies, waits for them, and re-layouts  17 us (2%)
  between operations  14.7 us (2%)
    psum x5, waiting for transfers between devices, from_root(): return lax.psum(jnp.where(is_root, value, jnp.zeros_like(value)), axes)  388 us
    all_to_all x2, waiting for transfers between devices, shards(): lax.all_to_all(sending.reshape(col_count, cap_incoming * BLK, BLK), 'col'...  112 us
    pallas_call x2, Pallas kernels, inverse_factor_of(): pl.pallas_call(inverse_kernel, out_shape=jax.ShapeDtypeStruct((width, wid...  91.9 us
    ppermute x2, waiting for transfers between devices, shift_rows(): lax.ppermute(value, 'row', [(s, (s + step) % count) for s in range(count)])  89.3 us
    all_gather x1, waiting for transfers between devices, shards(): gathered = lax.all_gather(kept, 'col')  75.2 us
    pallas_call x1, Pallas kernels, extend_add(): pl.pallas_call(functools.partial(extend_add_kernel, cap_cols), grid_spec=...  27.1 us
    pallas_call x1, Pallas kernels, parent_schur_of(): pl.pallas_call(parent_schur_kernel, grid_spec=grid_spec, out_shape=jax.Sh...  23.8 us
  transfers between devices with their start and end apart: 15, of which 13 were waited for; matrix products, arithmetic and copies ran while one was open for 2% of the time, Pallas kernels for 10%

profile of v1, /device:TPU:1, one launch (start us, length us, event | category | flops | bytes accessed | tf_op | source)
XLA Modules:
  0.0 953.3 jit_solution(16857495330230849361)
XLA Ops:
  7.2 2.3 slice_select_fusion.3
  9.6 0.7 multiply_add_fusion
  10.4 0.7 compare_bitcast_fusion
  11.1 0.2 convert_reduce_fusion.2
  11.5 0.2 fusion.21
  11.8 79.7 %all-reduce.6.cloned.1.call-done.block_ref = f32[512,512]{1,0:T(8,128)} async-done(((f32[512,512]{1,0:T(8,128)}), f32[512,512]{1,0:T(8,128)}) %all-reduce.6.cloned.1.call-update) | async-done | bytes 1048592 | tf_op jit(solution)/shard_map/psum | solution.py:17
  91.5 3.2 slice_select_fusion.1
  94.8 0.2 convert_reduce_fusion
  95.1 0.1 and_reduce_fusion
  95.2 0.2 fusion.18
  95.5 4.7 slice_select_fusion
  100.2 1.5 copy-done.3
  101.7 45.8 %inverse_factor.2 = f32[512,512]{1,0:T(8,128)S(1)} custom-call(f32[512,512]{1,0:T(8,128)S(1)} %copy-done.3), custom_call_target="tpu_custom_call" | custom-call | flops 60000002048 | bytes 2097152 | tf_op jit(solution)/shard_map/inverse_factor/pallas_call | solution.py:87
  147.5 15.7 %all-reduce.10.cloned.1.call-done = f32[512,1024]{1,0:T(8,128)} async-done(((f32[512,1024]{1,0:T(8,128)}), f32[512,1024]{1,0:T(8,128)}) %all-reduce.10.cloned.1.call-update) | async-done | bytes 2097168 | tf_op jit(solution)/shard_map/psum | solution.py:17
  163.2 3.5 fusion.46.cols_ref
  166.7 154.5 %all-reduce.8.cloned.1.call-done = f32[2048,512]{1,0:T(8,128)} async-done(((f32[2048,512]{1,0:T(8,128)}), f32[2048,512]{1,0:T(8,128)}) %all-reduce.8.cloned.1.call-update) | async-done | bytes 4194320 | tf_op jit(solution)/shard_map/psum | solution.py:17
  321.2 5.3 fusion.45.rows_ref
  326.5 17.6 %child_schur.1 = f32[2,2,8,128,512]{4,3,2,1,0:T(8,128)} custom-call(s32[16]{0:T(128)S(1)} %select_n.460.row_pick, s32[8]{0:T(128)S(1)} %select_n.464.col_pick, f32[2048,1024]{1,0:T(8,128)} %bitcast.109, f32[2048,512]{1,0:T(8,128)S(1)} %fusion.45.rows_ref, f32[512,1024]{1,0:T(8,128)S(1)} %fusion.46.cols_ref), custom_call_target="tpu_custom_call" | custom-call | tf_op jit(solution)/shard_map/child_schur/pallas_call | solution.py:149
  344.0 6.6 slice_bitcast_fusion
  350.7 1.4 collective-permute-start
  352.5 44.9 %collective-permute-done.refs_1_ = f32[8,128,512]{2,1,0:T(8,128)} collective-permute-done((f32[8,128,512]{2,1,0:T(8,128)}, f32[8,128,512]{2,1,0:T(8,128)}, u32[]{:S(2)}, u32[]{:S(2)}) %collective-permute-start) | collective-permute-done | bytes 2097184 | tf_op jit(solution)/shard_map/ppermute | solution.py:27
  397.4 1.6 copy-done.2
  399.0 7.8 squeeze_rows.2
  406.8 1.8 copy-done
  408.6 4.8 all-to-all-start
  413.4 1.4 collective-permute-start.1
  414.8 44.4 %collective-permute-done.1.refs_1_ = f32[8,128,512]{2,1,0:T(8,128)S(1)} collective-permute-done((f32[8,128,512]{2,1,0:T(8,128)}, f32[8,128,512]{2,1,0:T(8,128)S(1)}, u32[]{:S(2)}, u32[]{:S(2)}) %collective-permute-start.1) | collective-permute-done | bytes 2097184 | tf_op jit(solution)/shard_map/ppermute | solution.py:27
  459.2 1.4 squeeze_rows.3
  460.6 1.8 copy-done.1
  462.4 32.5 %all-to-all-done = f32[4,1792,128]{2,1,0:T(8,128)} async-done(((f32[4,1792,128]{2,1,0:T(8,128)}), f32[4,1792,128]{2,1,0:T(8,128)}, u32[]{:S(2)}, u32[]{:S(2)}) %all-to-all-start) | async-done | bytes 3670048 | tf_op jit(solution)/shard_map/all_to_all | solution.py:379
  494.9 4.8 all-to-all-start.1
  499.7 1.5 collective-permute-start.2
  501.3 79.9 %all-to-all-done.1 = f32[4,1792,128]{2,1,0:T(8,128)} async-done(((f32[4,1792,128]{2,1,0:T(8,128)}), f32[4,1792,128]{2,1,0:T(8,128)}, u32[]{:S(2)}, u32[]{:S(2)}) %all-to-all-start.1) | async-done | bytes 3670048 | tf_op jit(solution)/shard_map/all_to_all | solution.py:379
  581.1 1.5 collective-permute-start.3
  583.0 0.2 convert_reduce_fusion.3
  583.5 0.1 and_reduce_fusion.2
  583.6 0.2 convert_reduce_fusion.1
  584.0 0.2 fusion.16
  584.3 4.7 collective-permute-done.3.refs_3_
  589.0 27.1 %extend_add.1.front_ref = f32[4096,1024]{1,0:T(8,128)} custom-call(s32[64]{0:T(128)S(1)} %reshape.747.row_from, s32[32]{0:T(128)S(1)} %reshape.748.col_from, bf16[4096,1024]{1,0:T(8,128)(2,1)} %front_ref.1, f32[4,14,128,128]{3,2,1,0:T(8,128)} %bitcast.26.refs_0_, f32[4,14,128,128]{3,2,1,0:T(8,128)} %bitcast.30.refs_1_, ...), custom_call_target="tpu_custom_call" | custom-call | tf_op jit(solution)/shard_map/extend_add/pallas_call | solution.py:268
  616.1 2.3 slice_select_fusion.2
  618.5 76.2 %all-reduce.12.cloned.1.call-done = f32[512,512]{1,0:T(8,128)} async-done(((f32[512,512]{1,0:T(8,128)}), f32[512,512]{1,0:T(8,128)}) %all-reduce.12.cloned.1.call-update) | async-done | bytes 1048592 | tf_op jit(solution)/shard_map/psum | solution.py:17
  694.6 1.4 collective-permute-start.4
  696.0 1.7 slice.51
  697.7 0.9 collective-permute-done.4
  698.6 1.4 broadcast_select_fusion.3.block_ref
  700.1 1.5 broadcast_select_fusion.2
  701.6 0.3 all-gather.3.cloned.1.call-start
  701.8 61.9 %all-reduce.14.cloned.1.call-done = f32[512,1024]{1,0:T(8,128)} async-done(((f32[512,1024]{1,0:T(8,128)}), f32[512,1024]{1,0:T(8,128)}) %all-reduce.14.cloned.1.call-update) | async-done | bytes 2097168 | tf_op jit(solution)/shard_map/psum | solution.py:17
  763.7 2.7 slice_select_fusion.4
  766.4 0.7 collective-permute-start.5
  767.1 2.5 collective-permute-done.5
  769.6 2.8 select_select_fusion
  772.5 5.3 convolution_bitcast_fusion
  777.8 75.2 %all-gather.3.cloned.1.call-done = f32[1024,1024]{1,0:T(8,128)} async-done(((f32[256,1024]{1,0:T(8,128)}), f32[1024,1024]{1,0:T(8,128)}) %all-gather.3.cloned.1.call-update) | async-done | bytes 4194320 | tf_op jit(solution)/shard_map/all_gather | solution.py:402
  853.0 0.7 collective-permute-start.6
  853.7 46.1 %inverse_factor.3 = f32[512,512]{1,0:T(8,128)S(1)} custom-call(f32[512,512]{1,0:T(8,128)S(1)} %broadcast_select_fusion.3.block_ref), custom_call_target="tpu_custom_call" | custom-call | flops 60000002048 | bytes 2097152 | tf_op jit(solution)/shard_map/inverse_factor/pallas_call | solution.py:87
  899.8 1.9 fusion.47.cols_ref
  901.7 0.3 copy-done.5
  902.0 1.9 broadcast_select_fusion.1
  903.9 14.3 %fusion = f32[4,1024,512]{2,1,0:T(8,128)S(1)} fusion(f32[4,256,1024]{2,1,0:T(8,128)S(1)} %get-tuple-element.30, f32[4,256,1024]{2,1,0:T(8,128)S(1)} %get-tuple-element.29, f32[512,512]{1,0:T(8,128)S(1)} %inverse_factor.3), kind=kOutput, calls=%fused_computation.1 | convolution fusion | flops 6444548096 | bytes 17825792 | tf_op jit(solution)/shard_map/cks,pk->csp/dot_general | solution.py:413
  918.2 3.2 fusion.2
  921.4 1.0 copy.16
  922.5 23.8 %parent_schur.1 = f32[4096,1024]{1,0:T(8,128)} custom-call(s32[2]{0:T(128)S(1)} %pad_add_fusion.3.starts, f32[4096,1024]{1,0:T(8,128)} %extend_add.1.front_ref, f32[4096,512]{1,0:T(8,128)S(1)} %bitcast.103, f32[512,1024]{1,0:T(8,128)S(1)} %fusion.47.cols_ref), custom_call_target="tpu_custom_call" | custom-call | tf_op jit(solution)/shard_map/parent_schur/pallas_call | solution.py:194
  (69 shorter events, 2.4 us)
Async XLA Ops:
  7.2 84.3 %all-reduce.6.cloned.1.call-start = ((), (), s32[]{:S(2)}) async-start(), calls=%async_computation.2 | async-start | bytes 2097152 | tf_op jit(solution)/shard_map/psum | solution.py:17
  9.5 153.7 %all-reduce.10.cloned.1.call-start = ((), (), s32[]{:S(2)}) async-start(), calls=%async_computation.4 | async-start | bytes 4194304 | tf_op jit(solution)/shard_map/psum | solution.py:17
  94.7 226.5 %all-reduce.8.cloned.1.call-start = ((), (), s32[]{:S(2)}) async-start(), calls=%async_computation.3 | async-start | bytes 8388608 | tf_op jit(solution)/shard_map/psum | solution.py:17
  100.2 1.5 copy-start.3
  350.7 46.8 %collective-permute-start = (f32[8,128,512]{2,1,0:T(8,128)}, f32[8,128,512]{2,1,0:T(8,128)}, u32[]{:S(2)}, u32[]{:S(2)}) collective-permute-start(f32[8,128,512]{2,1,0:T(8,128)} %get-tuple-element.33), channel_id=1, source_target_pairs={{0,4},{4,0},{1,5},{5,1},{2,6},{6,2},{3,7},{7,3},{8,12},{12,8},{9,1... | collective-permute-start | bytes 6291464 | tf_op jit(solution)/shard_map/ppermute | solution.py:27
  397.4 1.6 copy-start.2
  406.8 1.8 copy-start
  408.6 86.2 %all-to-all-start = ((f32[4,1792,128]{2,1,0:T(8,128)}), f32[4,1792,128]{2,1,0:T(8,128)}, u32[]{:S(2)}, u32[]{:S(2)}) async-start(f32[4,1792,128]{2,1,0:T(8,128)} %bitcast.104), calls=%async_computation | async-start | bytes 7340032 | tf_op jit(solution)/shard_map/all_to_all | solution.py:379
  413.4 45.8 %collective-permute-start.1 = (f32[8,128,512]{2,1,0:T(8,128)}, f32[8,128,512]{2,1,0:T(8,128)S(1)}, u32[]{:S(2)}, u32[]{:S(2)}) collective-permute-start(f32[8,128,512]{2,1,0:T(8,128)} %get-tuple-element.31), channel_id=1, source_target_pairs={{0,4},{4,0},{1,5},{5,1},{2,6},{6,2},{3,7},{7,3},{8,12},{12,8},{9,1... | collective-permute-start | bytes 6291464 | tf_op jit(solution)/shard_map/ppermute | solution.py:27
  460.6 1.8 copy-start.1
  494.9 86.3 %all-to-all-start.1 = ((f32[4,1792,128]{2,1,0:T(8,128)}), f32[4,1792,128]{2,1,0:T(8,128)}, u32[]{:S(2)}, u32[]{:S(2)}) async-start(f32[4,1792,128]{2,1,0:T(8,128)} %bitcast.105), calls=%async_computation.1 | async-start | bytes 7340032 | tf_op jit(solution)/shard_map/all_to_all | solution.py:379
  499.7 194.9 %all-reduce.12.cloned.1.call-start = ((), (), s32[]{:S(2)}) async-start(), calls=%async_computation.5 | async-start | bytes 2097152 | tf_op jit(solution)/shard_map/psum | solution.py:17
  499.7 84.5 %collective-permute-start.2 = (f32[4,14,128,128]{3,2,1,0:T(8,128)}, f32[4,14,128,128]{3,2,1,0:T(8,128)}, u32[]{:S(2)}, u32[]{:S(2)}) collective-permute-start(f32[4,14,128,128]{3,2,1,0:T(8,128)} %bitcast.26.refs_0_), channel_id=1, source_target_pairs={{0,8},{8,0},{16,24},{24,16},{1,9},{9,1},{17,25},{25,17},{2,10},{10... | collective-permute-start | bytes 11010056 | tf_op jit(solution)/shard_map/ppermute | solution.py:22
  581.1 7.8 collective-permute-start.3
  618.4 145.3 %all-reduce.14.cloned.1.call-start = ((), (), s32[]{:S(2)}) async-start(), calls=%async_computation.6 | async-start | bytes 4194304 | tf_op jit(solution)/shard_map/psum | solution.py:17
  694.6 4.0 copy-start.6
  694.6 4.0 collective-permute-start.4
  701.6 151.5 %all-gather.3.cloned.1.call-start = ((), (), s32[]{:S(2)}) async-start(), calls=%async_computation.7 | async-start | bytes 5242880 | tf_op jit(solution)/shard_map/all_gather | solution.py:402
  766.4 3.2 collective-permute-start.5
  853.0 46.8 %copy-start.4 = (f32[512,1024]{1,0:T(8,128)S(1)}, f32[512,1024]{1,0:T(8,128)}, u32[]{:S(2)}) copy-start(f32[512,1024]{1,0:T(8,128)} %all-reduce.14.cloned.1.call-done) | copy-start | bytes 6291460
  853.0 48.7 %collective-permute-start.6 = (f32[4,256,1024]{2,1,0:T(8,128)}, f32[4,256,1024]{2,1,0:T(8,128)S(1)}, u32[]{:S(2)}, u32[]{:S(2)}) collective-permute-start(f32[4,256,1024]{2,1,0:T(8,128)} %bitcast.110), channel_id=1, source_target_pairs={{0,8},{8,0},{16,24},{24,16},{1,9},{9,1},{17,25},{25,17},{2,10},{10... | collective-permute-start | bytes 12582920 | tf_op jit(solution)/shard_map/ppermute | solution.py:22
  899.8 2.2 copy-start.5
Sparse Core Ops, SparseCore 0:
  12.1 79.3 all-reduce.5
  94.8 68.3 all-reduce.9
  166.2 154.9 all-reduce.7
  618.5 76.0 all-reduce.11
  701.7 61.9 all-reduce.13
  772.5 80.4 all-gather.2

commit v2 on v1

--- a/solution.py
+++ b/solution.py
@@ -25,6 +25,13 @@
 def shift_rows(value, step):
     count = lax.axis_size("row")
     return lax.ppermute(value, "row", [(s, (s + step) % count) for s in range(count)])
+
+
+def from_first_row(value):
+    at_first = lax.axis_index("row") == 0
+    if lax.axis_size("row") != 2:
+        return from_root(value, "row", at_first)
+    return jnp.where(at_first, value, lax.ppermute(value, "row", [(0, 1)]))
 
 
 def params():
@@ -296,12 +303,12 @@
     child_block = child_front[0]
     child_rows, child_cols = child_block.shape
     width = child_cols // 2
-    at_corner = (row_id == 0) & (col_id == 0)
-    diagonal = from_root(child_block[:width, :width], ("row", "col"), at_corner)
-    child_block, diagonal = lax.optimization_barrier((child_block, diagonal))
-    slab = from_root(child_block[:, :width], "col", col_id == 0)
-    top = from_root(child_block[:width], "row", row_id == 0)
-    inverse = inverse_factor_of(diagonal)
+    top = from_first_row(child_block[:width])
+    slab_head = from_root(child_block[:width, :width], "col", col_id == 0)
+    slab_rest, slab_head = lax.optimization_barrier((child_block[width:, :width], slab_head))
+    slab_rest = from_root(slab_rest, "col", col_id == 0)
+    inverse = inverse_factor_of(from_first_row(slab_head))
+    slab = jnp.concatenate((slab_head, slab_rest), axis=0)
     cols_factor = jnp.dot(inverse, top, precision=HIGH)
     rows_factor = jnp.dot(slab, inverse.T, precision=HIGH)
     out_width = width // col_count
@@ -388,12 +395,10 @@
     assembled = extend_add(parent_front, own_pieces + pair_pieces, row_from, col_from)
 
     parent_width = parent_cols // 2
-    corner = from_root(
-        assembled[:parent_width, :parent_width], ("row", "col"), at_corner
-    )
-    corner = jnp.where(own_half == 0, corner, pair_swap(corner))
-    strip, corner = lax.optimization_barrier((assembled[:parent_width], corner))
-    parent_top = from_root(strip, "row", row_id == 0)
+    parent_top = from_first_row(assembled[:parent_width])
+    corner = from_root(assembled[:parent_width, :parent_width], "col", col_id == 0)
+    parent_top, corner = lax.optimization_barrier((parent_top, corner))
+    corner = from_first_row(jnp.where(own_half == 0, corner, pair_swap(corner)))
     if row_count == 2:
         part = parent_width // 2
         kept = jnp.where(own_half == 0, parent_top[:part], parent_top[part:])

time: 965 us -> 749 us (0.78)
  waiting for transfers between devices: 673 us -> 442 us
  starting transfers between devices: 18.5 us -> 33 us
    psum x5 -> x3, waiting for transfers between devices: 388 us -> 104 us  [from_root(): return lax.psum(jnp.where(is_root, value, jnp.zeros_like(value)), axes)]
    ppermute x0 -> x4, waiting for transfers between devices: none -> 71.7 us  [from_first_row(): return jnp.where(at_first, value, lax.ppermute(value, 'row', [(0, 1)]))]
    all_gather x1, waiting for transfers between devices: 75.2 us -> 52.7 us  [shards(): gathered = lax.all_gather(kept, 'col')]
    ppermute x0 -> x4, starting transfers between devices: none -> 17.9 us  [from_first_row(): return jnp.where(at_first, value, lax.ppermute(value, 'row', [(0, 1)]))]
  transfers between devices with their start and end apart: 15 -> 17, of which waited for: 13 -> 14; matrix products, arithmetic and copies ran while one was open for 2% -> 4% of each run, Pallas kernels for 10% -> 13%
where the time goes in v2:
time: 749 us; the launch traced here: 738 us
  waiting for transfers between devices  442 us (59%)
  Pallas kernels  170 us (23%)
  matrix products  33.8 us (5%)
  starting transfers between devices  33 us (4%)
  local copies, waits for them, and re-layouts  25.2 us (3%)
  other arithmetic  20.7 us (3%)
  between operations  14.4 us (2%)
    all_to_all x2, waiting for transfers between devices, shards(): lax.all_to_all(sending.reshape(col_count, cap_incoming * BLK, BLK), 'col'...  112 us
    psum x3, waiting for transfers between devices, from_root(): return lax.psum(jnp.where(is_root, value, jnp.zeros_like(value)), axes)  104 us
    pallas_call x2, Pallas kernels, inverse_factor_of(): pl.pallas_call(inverse_kernel, out_shape=jax.ShapeDtypeStruct((width, wid...  92 us
    ppermute x2, waiting for transfers between devices, shift_rows(): lax.ppermute(value, 'row', [(s, (s + step) % count) for s in range(count)])  91.1 us
    ppermute x4, waiting for transfers between devices, from_first_row(): return jnp.where(at_first, value, lax.ppermute(value, 'row', [(0, 1)]))  71.7 us
    all_gather x1, waiting for transfers between devices, shards(): gathered = lax.all_gather(kept, 'col')  52.7 us
    pallas_call x1, Pallas kernels, extend_add(): pl.pallas_call(functools.partial(extend_add_kernel, cap_cols), grid_spec=...  27.1 us
    pallas_call x1, Pallas kernels, parent_schur_of(): pl.pallas_call(parent_schur_kernel, grid_spec=grid_spec, out_shape=jax.Sh...  23.8 us
  transfers between devices with their start and end apart: 17, of which 14 were waited for; matrix products, arithmetic and copies ran while one was open for 4% of the time, Pallas kernels for 13%

profile of v2, /device:TPU:1, one launch (start us, length us, event | category | flops | bytes accessed | tf_op | source)
XLA Modules:
  0.0 738.4 jit_solution(10489170410164006719)
XLA Ops:
  7.2 2.3 slice_select_fusion.1
  9.6 1.7 slice_bitcast_fusion.4
  11.3 5.4 collective-permute-start.1
  16.9 0.2 convert_reduce_fusion.2
  17.3 4.0 slice.50
  21.2 0.2 convert_reduce_fusion
  21.8 43.4 %all-reduce.4.cloned.1.call-done = f32[512,512]{1,0:T(8,128)} async-done(((f32[512,512]{1,0:T(8,128)}), f32[512,512]{1,0:T(8,128)}) %all-reduce.4.cloned.1.call-update) | async-done | bytes 1048592 | tf_op jit(solution)/shard_map/psum | solution.py:17
  65.2 4.1 collective-permute-start
  69.8 4.0 broadcast_select_fusion.2
  73.8 16.9 %collective-permute-done = f32[512,512]{1,0:T(8,128)} collective-permute-done((f32[512,512]{1,0:T(8,128)}, f32[512,512]{1,0:T(8,128)}, u32[]{:S(2)}, u32[]{:S(2)}) %collective-permute-start) | collective-permute-done | bytes 1048608 | tf_op jit(solution)/shard_map/ppermute | solution.py:34
  90.7 1.2 broadcast_select_fusion.6
  91.9 46.0 %inverse_factor.2 = f32[512,512]{1,0:T(8,128)S(1)} custom-call(f32[512,512]{1,0:T(8,128)S(1)} %get-tuple-element.35.block_ref), custom_call_target="tpu_custom_call" | custom-call | flops 60000002048 | bytes 2097152 | tf_op jit(solution)/shard_map/inverse_factor/pallas_call | solution.py:94
  138.0 3.5 fusion.2.cols_ref
  141.5 53.5 %all-reduce.6.cloned.1.call-done = f32[1536,512]{1,0:T(8,128)} async-done(((f32[1536,512]{1,0:T(8,128)}), f32[1536,512]{1,0:T(8,128)}) %all-reduce.6.cloned.1.call-update) | async-done | bytes 3145744 | tf_op jit(solution)/shard_map/psum | solution.py:17
  195.0 3.8 constant_dynamic-update-slice_fusion
  198.8 5.3 fusion.48.rows_ref
  204.1 17.6 %child_schur.1 = f32[2,2,8,128,512]{4,3,2,1,0:T(8,128)} custom-call(s32[16]{0:T(128)S(1)} %select_n.474.row_pick, s32[8]{0:T(128)S(1)} %select_n.478.col_pick, f32[2048,1024]{1,0:T(8,128)} %bitcast.112, f32[2048,512]{1,0:T(8,128)S(1)} %fusion.48.rows_ref, f32[512,1024]{1,0:T(8,128)S(1)} %fusion.2.cols_ref), custom_call_target="tpu_custom_call" | custom-call | tf_op jit(solution)/shard_map/child_schur/pallas_call | solution.py:156
  221.7 6.8 slice_bitcast_fusion
  228.5 0.8 collective-permute-start.2
  229.8 45.5 %collective-permute-done.2.refs_1_ = f32[8,128,512]{2,1,0:T(8,128)} collective-permute-done((f32[8,128,512]{2,1,0:T(8,128)}, f32[8,128,512]{2,1,0:T(8,128)}, u32[]{:S(2)}, u32[]{:S(2)}) %collective-permute-start.2) | collective-permute-done | bytes 2097184 | tf_op jit(solution)/shard_map/ppermute | solution.py:27
  275.3 1.6 copy-done.2
  276.9 7.8 %squeeze_rows.2 = f32[4,14,128,128]{3,2,1,0:T(8,128)S(1)} custom-call(s32[28]{0:T(128)S(1)} %reshape.750.source, f32[8,128,512]{2,1,0:T(8,128)S(1)} %copy-done.2, f32[8,128,512]{2,1,0:T(8,128)} %collective-permute-done.2.refs_1_), custom_call_target="tpu_custom_call" | custom-call | tf_op jit(solution)/shard_map/squeeze_rows/pallas_call | solution.py:231
  284.7 1.8 copy-done
  286.6 4.8 all-to-all-start
  291.3 0.3 collective-permute-start.3
  291.6 45.6 %collective-permute-done.3.refs_1_ = f32[8,128,512]{2,1,0:T(8,128)S(1)} collective-permute-done((f32[8,128,512]{2,1,0:T(8,128)}, f32[8,128,512]{2,1,0:T(8,128)S(1)}, u32[]{:S(2)}, u32[]{:S(2)}) %collective-permute-start.3) | collective-permute-done | bytes 2097184 | tf_op jit(solution)/shard_map/ppermute | solution.py:27
  337.2 1.4 squeeze_rows.3
  338.6 1.8 copy-done.1
  340.4 32.4 %all-to-all-done = f32[4,1792,128]{2,1,0:T(8,128)} async-done(((f32[4,1792,128]{2,1,0:T(8,128)}), f32[4,1792,128]{2,1,0:T(8,128)}, u32[]{:S(2)}, u32[]{:S(2)}) %all-to-all-start) | async-done | bytes 3670048 | tf_op jit(solution)/shard_map/all_to_all | solution.py:386
  372.8 4.8 all-to-all-start.1
  377.7 1.5 collective-permute-start.4
  379.2 79.9 %all-to-all-done.1 = f32[4,1792,128]{2,1,0:T(8,128)} async-done(((f32[4,1792,128]{2,1,0:T(8,128)}), f32[4,1792,128]{2,1,0:T(8,128)}, u32[]{:S(2)}, u32[]{:S(2)}) %all-to-all-start.1) | async-done | bytes 3670048 | tf_op jit(solution)/shard_map/all_to_all | solution.py:386
  459.1 1.5 collective-permute-start.5
  460.9 0.2 convert_reduce_fusion.3
  461.5 0.2 convert_reduce_fusion.1
  461.9 0.2 fusion.19
  462.2 4.7 collective-permute-done.5.refs_3_
  466.9 27.1 %extend_add.1.front_ref = f32[4096,1024]{1,0:T(8,128)} custom-call(s32[64]{0:T(128)S(1)} %reshape.748.row_from, s32[32]{0:T(128)S(1)} %reshape.749.col_from, bf16[4096,1024]{1,0:T(8,128)(2,1)} %front_ref.1, f32[4,14,128,128]{3,2,1,0:T(8,128)} %bitcast.27.refs_0_, f32[4,14,128,128]{3,2,1,0:T(8,128)} %bitcast.31.refs_1_, ...), custom_call_target="tpu_custom_call" | custom-call | tf_op jit(solution)/shard_map/extend_add/pallas_call | solution.py:275
  494.0 1.7 slice.56
  495.7 4.2 collective-permute-start.6
  499.9 2.3 slice_select_fusion
  502.2 40.9 %collective-permute-done.6 = f32[512,1024]{1,0:T(8,128)} collective-permute-done((f32[512,1024]{1,0:T(8,128)S(1)}, f32[512,1024]{1,0:T(8,128)}, u32[]{:S(2)}, u32[]{:S(2)}) %collective-permute-start.6) | collective-permute-done | bytes 2097184 | tf_op jit(solution)/shard_map/ppermute | solution.py:34
  543.2 2.0 broadcast_select_fusion.3
  545.2 6.6 all-reduce.8.cloned.1.call-done
  551.8 1.1 slice_select_fusion.2
  552.9 0.5 collective-permute-start.9
  553.4 2.6 collective-permute-done.9
  556.0 2.5 select_select_fusion
  558.6 2.9 collective-permute-done.7
  561.4 0.2 broadcast_select_fusion.4
  561.7 4.3 collective-permute-start.8
  566.1 5.6 convolution_bitcast_fusion
  571.7 13.9 %collective-permute-done.8 = f32[512,512]{1,0:T(8,128)} collective-permute-done((f32[512,512]{1,0:T(8,128)S(1)}, f32[512,512]{1,0:T(8,128)}, u32[]{:S(2)}, u32[]{:S(2)}) %collective-permute-start.8) | collective-permute-done | bytes 1048608 | tf_op jit(solution)/shard_map/ppermute | solution.py:34
  585.6 0.2 broadcast_select_fusion.5.block_ref
  585.8 52.7 %all-gather.3.cloned.1.call-done = f32[1024,1024]{1,0:T(8,128)} async-done(((f32[256,1024]{1,0:T(8,128)}), f32[1024,1024]{1,0:T(8,128)}) %all-gather.3.cloned.1.call-update) | async-done | bytes 4194320 | tf_op jit(solution)/shard_map/all_gather | solution.py:407
  638.5 0.7 collective-permute-start.10
  639.2 46.0 %inverse_factor.3 = f32[512,512]{1,0:T(8,128)S(1)} custom-call(f32[512,512]{1,0:T(8,128)S(1)} %broadcast_select_fusion.5.block_ref), custom_call_target="tpu_custom_call" | custom-call | flops 60000002048 | bytes 2097152 | tf_op jit(solution)/shard_map/inverse_factor/pallas_call | solution.py:94
  685.2 1.9 fusion.49.cols_ref
  687.1 0.3 copy-done.5
  687.4 1.9 broadcast_select_fusion.1
  689.3 14.3 %fusion = f32[4,1024,512]{2,1,0:T(8,128)S(1)} fusion(f32[4,256,1024]{2,1,0:T(8,128)S(1)} %get-tuple-element.30, f32[4,256,1024]{2,1,0:T(8,128)S(1)} %get-tuple-element.29, f32[512,512]{1,0:T(8,128)S(1)} %inverse_factor.3), kind=kOutput, calls=%fused_computation.1 | convolution fusion | flops 6444548096 | bytes 17825792 | tf_op jit(solution)/shard_map/cks,pk->csp/dot_general | solution.py:418
  703.6 3.2 fusion.4
  706.8 1.0 copy.16
  707.9 23.8 %parent_schur.1 = f32[4096,1024]{1,0:T(8,128)} custom-call(s32[2]{0:T(128)S(1)} %pad_add_fusion.3.starts, f32[4096,1024]{1,0:T(8,128)} %extend_add.1.front_ref, f32[4096,512]{1,0:T(8,128)S(1)} %bitcast.107, f32[512,1024]{1,0:T(8,128)S(1)} %fusion.49.cols_ref), custom_call_target="tpu_custom_call" | custom-call | tf_op jit(solution)/shard_map/parent_schur/pallas_call | solution.py:201
  (76 shorter events, 3.0 us)
Async XLA Ops:
  7.2 9.6 %copy-start.7 = (s32[4,28]{1,0:T(4,128)S(1)}, s32[4,28]{1,0:T(4,128)}, u32[]{:S(2)}) copy-start(s32[4,28]{1,0:T(4,128)} %param.5) | copy-start | bytes 1348
  7.2 58.1 %all-reduce.4.cloned.1.call-start = ((), (), s32[]{:S(2)}) async-start(), calls=%async_computation.2 | async-start | bytes 2097152 | tf_op jit(solution)/shard_map/psum | solution.py:17
  9.5 185.5 %all-reduce.6.cloned.1.call-start = ((), (), s32[]{:S(2)}) async-start(), calls=%async_computation.3 | async-start | bytes 6291456 | tf_op jit(solution)/shard_map/psum | solution.py:17
  11.3 126.6 %collective-permute-start.1 = (f32[512,1024]{1,0:T(8,128)S(1)}, f32[512,1024]{1,0:T(8,128)}, u32[]{:S(2)}, u32[]{:S(2)}) collective-permute-start(f32[512,1024]{1,0:T(8,128)S(1)} %slice_bitcast_fusion.4), channel_id=1, source_target_pairs={{0,4},{1,5},{2,6},{3,7},{8,12},{9,13},{10,14},{11,15},{16,20},{17,... | collective-permute-start | bytes 6291464 | tf_op jit(solution)/shard_map/ppermute | solution.py:34
  65.2 25.5 %collective-permute-start = (f32[512,512]{1,0:T(8,128)}, f32[512,512]{1,0:T(8,128)}, u32[]{:S(2)}, u32[]{:S(2)}) collective-permute-start(f32[512,512]{1,0:T(8,128)} %all-reduce.4.cloned.1.call-done), channel_id=1, source_target_pairs={{0,4},{1,5},{2,6},{3,7},{8,12},{9,13},{10,14},{11,15},{16,20},{17,... | collective-permute-start | bytes 3145736 | tf_op jit(solution)/shard_map/ppermute | solution.py:34
  69.8 20.9 %copy-start.6 = (f32[512,512]{1,0:T(8,128)S(1)}, f32[512,512]{1,0:T(8,128)}, u32[]{:S(2)}) copy-start(f32[512,512]{1,0:T(8,128)} %all-reduce.4.cloned.1.call-done) | copy-start | bytes 3145732
  228.5 46.8 %collective-permute-start.2 = (f32[8,128,512]{2,1,0:T(8,128)}, f32[8,128,512]{2,1,0:T(8,128)}, u32[]{:S(2)}, u32[]{:S(2)}) collective-permute-start(f32[8,128,512]{2,1,0:T(8,128)} %get-tuple-element.33), channel_id=1, source_target_pairs={{0,4},{4,0},{1,5},{5,1},{2,6},{6,2},{3,7},{7,3},{8,12},{12,8},{9,1... | collective-permute-start | bytes 6291464 | tf_op jit(solution)/shard_map/ppermute | solution.py:27
  275.3 1.6 copy-start.2
  284.7 1.8 copy-start
  286.6 86.2 %all-to-all-start = ((f32[4,1792,128]{2,1,0:T(8,128)}), f32[4,1792,128]{2,1,0:T(8,128)}, u32[]{:S(2)}, u32[]{:S(2)}) async-start(f32[4,1792,128]{2,1,0:T(8,128)} %bitcast.108), calls=%async_computation | async-start | bytes 7340032 | tf_op jit(solution)/shard_map/all_to_all | solution.py:386
  291.3 45.9 %collective-permute-start.3 = (f32[8,128,512]{2,1,0:T(8,128)}, f32[8,128,512]{2,1,0:T(8,128)S(1)}, u32[]{:S(2)}, u32[]{:S(2)}) collective-permute-start(f32[8,128,512]{2,1,0:T(8,128)} %get-tuple-element.31), channel_id=1, source_target_pairs={{0,4},{4,0},{1,5},{5,1},{2,6},{6,2},{3,7},{7,3},{8,12},{12,8},{9,1... | collective-permute-start | bytes 6291464 | tf_op jit(solution)/shard_map/ppermute | solution.py:27
  338.6 1.8 copy-start.1
  372.8 86.3 %all-to-all-start.1 = ((f32[4,1792,128]{2,1,0:T(8,128)}), f32[4,1792,128]{2,1,0:T(8,128)}, u32[]{:S(2)}, u32[]{:S(2)}) async-start(f32[4,1792,128]{2,1,0:T(8,128)} %bitcast.109), calls=%async_computation.1 | async-start | bytes 7340032 | tf_op jit(solution)/shard_map/all_to_all | solution.py:386
  377.6 174.2 %all-reduce.8.cloned.1.call-start = ((), (), s32[]{:S(2)}) async-start(), calls=%async_computation.4 | async-start | bytes 2097152 | tf_op jit(solution)/shard_map/psum | solution.py:17
  377.7 84.5 %collective-permute-start.4 = (f32[4,14,128,128]{3,2,1,0:T(8,128)}, f32[4,14,128,128]{3,2,1,0:T(8,128)}, u32[]{:S(2)}, u32[]{:S(2)}) collective-permute-start(f32[4,14,128,128]{3,2,1,0:T(8,128)} %bitcast.27.refs_0_), channel_id=1, source_target_pairs={{0,8},{8,0},{16,24},{24,16},{1,9},{9,1},{17,25},{25,17},{2,10},{10... | collective-permute-start | bytes 11010056 | tf_op jit(solution)/shard_map/ppermute | solution.py:22
  459.1 7.8 %collective-permute-start.5 = (f32[4,14,128,128]{3,2,1,0:T(8,128)}, f32[4,14,128,128]{3,2,1,0:T(8,128)}, u32[]{:S(2)}, u32[]{:S(2)}) collective-permute-start(f32[4,14,128,128]{3,2,1,0:T(8,128)} %bitcast.31.refs_1_), channel_id=1, source_target_pairs={{0,8},{8,0},{16,24},{24,16},{1,9},{9,1},{17,25},{25,17},{2,10},{10... | collective-permute-start | bytes 11010056 | tf_op jit(solution)/shard_map/ppermute | solution.py:22
  495.7 47.5 %collective-permute-start.6 = (f32[512,1024]{1,0:T(8,128)S(1)}, f32[512,1024]{1,0:T(8,128)}, u32[]{:S(2)}, u32[]{:S(2)}) collective-permute-start(f32[512,1024]{1,0:T(8,128)S(1)} %slice.56), channel_id=1, source_target_pairs={{0,4},{1,5},{2,6},{3,7},{8,12},{9,13},{10,14},{11,15},{16,20},{17,... | collective-permute-start | bytes 6291464 | tf_op jit(solution)/shard_map/ppermute | solution.py:34
  502.2 136.3 %all-gather.3.cloned.1.call-start = ((), (), s32[]{:S(2)}) async-start(), calls=%async_computation.5 | async-start | bytes 5242880 | tf_op jit(solution)/shard_map/all_gather | solution.py:407
  545.2 13.3 %copy-start.3 = (f32[512,1024]{1,0:T(8,128)}, f32[512,1024]{1,0:T(8,128)S(1)}, u32[]{:S(2)}) copy-start(f32[512,1024]{1,0:T(8,128)S(1)} %broadcast_select_fusion.3) | copy-start | bytes 6291460
  552.9 3.1 collective-permute-start.9
  558.5 2.9 collective-permute-start.7
  561.7 23.9 %collective-permute-start.8 = (f32[512,512]{1,0:T(8,128)S(1)}, f32[512,512]{1,0:T(8,128)}, u32[]{:S(2)}, u32[]{:S(2)}) collective-permute-start(f32[512,512]{1,0:T(8,128)S(1)} %broadcast_select_fusion.4), channel_id=1, source_target_pairs={{0,4},{1,5},{2,6},{3,7},{8,12},{9,13},{10,14},{11,15},{16,20},{17,... | collective-permute-start | bytes 3145736 | tf_op jit(solution)/shard_map/ppermute | solution.py:34
  638.5 46.7 %copy-start.4 = (f32[512,1024]{1,0:T(8,128)S(1)}, f32[512,1024]{1,0:T(8,128)}, u32[]{:S(2)}) copy-start(f32[512,1024]{1,0:T(8,128)} %copy-done.3) | copy-start | bytes 6291460
  638.5 48.6 %collective-permute-start.10 = (f32[4,256,1024]{2,1,0:T(8,128)}, f32[4,256,1024]{2,1,0:T(8,128)S(1)}, u32[]{:S(2)}, u32[]{:S(2)}) collective-permute-start(f32[4,256,1024]{2,1,0:T(8,128)} %bitcast.113), channel_id=1, source_target_pairs={{0,8},{8,0},{16,24},{24,16},{1,9},{9,1},{17,25},{25,17},{2,10},{10... | collective-permute-start | bytes 12582920 | tf_op jit(solution)/shard_map/ppermute | solution.py:22
  685.2 2.2 copy-start.5
Sparse Core Ops, SparseCore 0:
  10.9 54.2 all-reduce.3
  73.9 121.0 all-reduce.5
  502.3 49.4 all-reduce.7
  558.6 79.8 all-gather.2
